TPU v7x, 768 devices: a whole 4x8x12 slice. The times are simulated.
768 devices in a mesh: grp: 96 (over y, z), sub: 8 (over x, core).
Axes of the slice: x: 4, y: 8, z: 12, core: 2. Of those that a mesh axis runs over, the one named last changes fastest.
Arguments:
- multipoles: bfloat16 [786432, 128], P(('grp', 'sub')), may hold values from -6 to 6
- up_ops: bfloat16 [8, 128, 128], replicated, may hold values from -0.1875 to 0.1875
- down_ops: bfloat16 [8, 128, 128], replicated, may hold values from -0.5 to 0.5
- far_ops: bfloat16 [189, 128, 128], replicated, may hold values from -0.0390625 to 0.0390625
- sources5: int32 [189, 98304], P(None, ('grp', 'sub')), may hold values from -1 to 1407, as said below
- sources4: int32 [189, 12288], P(None, ('grp', 'sub')), may hold values from -1 to 127, as said below
- sources3: int32 [189, 1536], P(None, ('grp', 'sub')), may hold values from -1 to 1535, as said below
- send_boxes: int32 [768, 96, 4], P(('grp', 'sub')), may hold values from 0 to 127
- send_counts: int32 [768, 96], P(('grp', 'sub')), may hold values from 0 to 4, as said below
Outputs:
- local_six: float32 [786432, 128], P(('grp', 'sub'))
Inputs may be any that keep to these rules, and one draw needn't show every extreme that they name: `sources5`: -1 means no source of that class; smaller than 1024 names a block of the target group's level-5 boxes, otherwise the entry minus that is j * 4 + k, a slot received from grp index j. `sources4`: -1 means no source; otherwise a block of the target group's level-4 boxes. `sources3`: -1 means no source; otherwise a level-3 box. `send_counts`: in every draw one grp index receives 4 filled slots from every device.
All inputs are finite; a program needn't handle non-finite values.
Results may differ from a plain program's by a relative error of at most 0.012.
Values may be sent and summed in bfloat16 or wider, within the bound.
A program may use at most 64 MiB of HBM per device.

v0:
```python
import jax
import jax.numpy as jnp
from jax import lax
from jax.sharding import PartitionSpec as P


def ascend(children, up_ops):
    coeffs = children.shape[1]
    stacked = children.reshape(children.shape[0] // 8, 8 * coeffs)
    return jnp.dot(
        stacked, up_ops.reshape(8 * coeffs, coeffs), preferred_element_type=jnp.float32
    ).astype(jnp.bfloat16)


def descend(parent, down_ops):
    coeffs = parent.shape[1]
    spread = jnp.transpose(down_ops, (1, 0, 2)).reshape(coeffs, 8 * coeffs)
    return jnp.dot(parent, spread, preferred_element_type=jnp.float32).reshape(
        parent.shape[0] * 8, coeffs
    )


def far_sum(source_rows, sources, far_ops):
    lookup = sources.T
    picked = source_rows[jnp.maximum(lookup, 0)]
    picked = jnp.where((lookup >= 0)[:, :, None], picked, jnp.zeros((), source_rows.dtype))
    flattened = picked.reshape(lookup.shape[0], lookup.shape[1] * source_rows.shape[1])
    operators = far_ops.reshape(far_ops.shape[0] * far_ops.shape[1], far_ops.shape[2])
    return jnp.dot(flattened, operators, preferred_element_type=jnp.float32)


def body(
    multipoles, up_ops, down_ops, far_ops, sources5, sources4, sources3, send_boxes, send_counts
):
    poles_five = ascend(multipoles, up_ops)
    poles_four = ascend(poles_five, up_ops)
    poles_three = ascend(poles_four, up_ops)
    chosen = send_boxes[0]
    sent_count = send_counts[0]
    slot_ids = jnp.arange(chosen.shape[1], dtype=jnp.int32)
    filled = slot_ids[None, :] < sent_count[:, None]
    packed = jnp.where(filled[:, :, None], poles_five[chosen], jnp.zeros((), poles_five.dtype))
    arrived = lax.all_to_all(packed, "grp", split_axis=0, concat_axis=0, tiled=True)
    group_five, group_four, group_three = (
        lax.all_gather(poles_five, "sub", axis=0, tiled=True),
        lax.all_gather(poles_four, "sub", axis=0, tiled=True),
        lax.all_gather(poles_three, "sub", axis=0, tiled=True),
    )
    global_tops = lax.all_gather(poles_three, ("grp", "sub"), axis=0, tiled=True)
    local_three = far_sum(global_tops, sources3, far_ops).astype(jnp.bfloat16)
    local_four = (descend(local_three, down_ops) + far_sum(group_four, sources4, far_ops)).astype(
        jnp.bfloat16
    )
    source_rows = jnp.concatenate([group_five, arrived.reshape(-1, poles_five.shape[1])], 0)
    local_five = (descend(local_four, down_ops) + far_sum(source_rows, sources5, far_ops)).astype(
        jnp.bfloat16
    )
    return descend(local_five, down_ops)


def solution(mesh):
    in_specs = (
        P(("grp", "sub"), None),
        P(),
        P(),
        P(),
        P(None, ("grp", "sub")),
        P(None, ("grp", "sub")),
        P(None, ("grp", "sub")),
        P(("grp", "sub"), None, None),
        P(("grp", "sub"), None),
    )
    out_specs = P(("grp", "sub"), None)
    return jax.shard_map(body, mesh=mesh, in_specs=in_specs, out_specs=out_specs, check_vma=False)
```

profile of v0, /device:TPU:1, one launch (start us, length us, event | category | flops | bytes accessed | tf_op | source)
XLA Modules:
  0.0 243.9 jit_solution(16063963142013305503)
XLA Ops:
  0.0 0.0 copy-start
  0.0 1.1 reshape.92
  1.1 0.7 compare_select_fusion
  1.8 0.1 copy.19
  1.9 0.1 reshape.119
  2.0 0.7 iota_compare_fusion
  2.8 0.0 copy-done
  2.8 0.2 convolution_convert_fusion
  3.0 1.4 gather_fusion.2
  4.5 0.8 broadcast_select_fusion.2
  5.3 22.6 %all-to-all-start = ((bf16[96,4,128]{2,1,0:T(4,128)(2,1)}), bf16[96,4,128]{2,1,0:T(4,128)(2,1)S(1)}, u32[]{:S(2)}, u32[]{:S(2)}) async-start(bf16[96,4,128]{2,1,0:T(4,128)(2,1)} %broadcast_select_fusion.2), calls=%async_computation | async-start | bytes 196608 | tf_op jit(solution)/shard_map/all_to_all | solution.py:43
  27.9 0.7 maximum_bitcast_fusion.2
  28.5 0.7 compare_bitcast_fusion.2
  29.2 0.1 convolution_convert_fusion.1
  29.4 13.9 %all_gather.10 = bf16[128,128]{1,0:T(8,128)(2,1)S(1)} all-gather(bf16[16,128]{1,0:T(8,128)(2,1)S(1)} %convolution_convert_fusion.1), channel_id=1, replica_groups=mesh['grp'=96,'sub'=8] {'sub'}, dimensions={0}, use_global_device_ids=true | all-gather | bytes 36864 | tf_op jit(solution)/shard_map/all_gather | solution.py:46
  43.3 0.7 maximum_bitcast_fusion.1
  44.0 0.7 compare_bitcast_fusion.1
  44.7 12.9 %all_gather.11 = bf16[1024,128]{1,0:T(8,128)(2,1)S(1)} all-gather(bf16[128,128]{1,0:T(8,128)(2,1)S(1)} %convolution_convert_fusion), channel_id=1, replica_groups=mesh['grp'=96,'sub'=8] {'sub'}, dimensions={0}, use_global_device_ids=true | all-gather | bytes 294912 | tf_op jit(solution)/shard_map/all_gather | solution.py:45
  57.6 0.9 maximum_bitcast_fusion
  58.5 0.9 compare_bitcast_fusion
  59.4 0.2 fusion.19
  59.6 88.6 %all-gather = bf16[768,2,128]{2,1,0:T(2,128)(2,1)S(1)} all-gather(bf16[1,2,128]{2,1,0:T(2,128)(2,1)S(1)} %fusion.19), channel_id=1, replica_groups=mesh['grp'=96,'sub'=8] {'grp','sub'}, dimensions={0}, use_global_device_ids=true | all-gather | bytes 393728 | tf_op jit(solution)/shard_map/all_gather | solution.py:49
  148.1 0.1 reshape.103
  148.2 1.4 gather_fusion
  149.7 1.1 copy.16
  150.9 0.1 broadcast_select_fusion.3
  151.0 3.9 %fusion.18 = f32[2,1024]{1,0:T(2,128)S(1)} fusion(bf16[128,1024]{0,1:T(8,128)(2,1)S(1)} %bitcast.64, bf16[189,128,128]{2,1,0:T(8,128)(2,1)} %param.12, bf16[2,189,128]{2,1,0:T(8,128)(2,1)S(1)} %broadcast_select_fusion.3), kind=kOutput, calls=%fused_computation.20 | convolution fusion | flops 12910848 | bytes 6560256 | tf_op jit(solution)/shard_map/dot_general | solution.py:18
  154.9 0.1 reshape.111
  155.1 9.3 %gather_fusion.1 = bf16[3024,128]{1,0:T(8,128)(2,1)S(1)} fusion(bf16[128,128]{1,0:T(8,128)(2,1)S(1)} %all_gather.10, s32[3072]{0:T(1024)S(1)} %pad_clamp_fusion.1), kind=kCustom, calls=%fused_computation.1 | custom fusion | bytes 1560384 | tf_op jit(solution)/shard_map/gather | solution.py:25
  164.4 0.2 reshape.110
  164.6 0.6 broadcast_select_fusion.1
  165.2 4.2 %fusion.16 = f32[16,1024]{1,0:T(8,128)S(1)} fusion(bf16[128,1024]{0,1:T(8,128)(2,1)S(1)} %bitcast.65, f32[16,128]{1,0:T(8,128)S(1)} %reshape.97, bf16[189,128,128]{2,1,0:T(8,128)(2,1)} %param.12, bf16[16,189,128]{2,1,0:T(8,128)(2,1)S(1)} %broadcast_select_fusion.1), kind=kOutput, calls=%fused_computation.16 | convolution fusion | flops 103288832 | bytes 7303168 | tf_op jit(solution)/shard_map/dot_general | solution.py:18
  169.5 0.1 copy.20
  169.6 0.3 reshape.127
  169.9 0.1 copy.18
  170.0 0.0 all-to-all-done
  170.1 49.4 %gather_fusion.3 = bf16[24192,128]{1,0:T(8,128)(2,1)} fusion(bf16[1408,128]{1,0:T(8,128)(2,1)S(1)} %pad_maximum_fusion, s32[24576]{0:T(1024)S(1)} %pad_clamp_fusion), kind=kCustom, calls=%fused_computation.3 | custom fusion | bytes 12483072 | tf_op jit(solution)/shard_map/gather | solution.py:25
  219.5 8.5 %reshape.126 = bf16[128,189,128]{2,1,0:T(8,128)(2,1)} reshape(bf16[24192,128]{1,0:T(8,128)(2,1)} %gather_fusion.3) | data formatting | bytes 12386304 | tf_op jit(solution)/shard_map/gather | solution.py:25
  228.0 6.4 %broadcast_select_fusion = bf16[128,189,128]{2,1,0:T(8,128)(2,1)} fusion(bf16[128,189,128]{2,1,0:T(8,128)(2,1)} %reshape.126, pred[128,189]{1,0:T(8,128)(4,1)S(1)} %copy.18), kind=kLoop, calls=%fused_computation.4 | loop fusion | flops 3096576 | bytes 12410496 | tf_op jit(solution)/shard_map/jit(_where)/select_n | solution.py:26
  234.4 8.6 %fusion.12 = f32[128,1024]{1,0:T(8,128)S(1)} fusion(bf16[128,1024]{0,1:T(8,128)(2,1)S(1)} %bitcast.66, f32[128,128]{1,0:T(8,128)S(1)} %reshape.98, bf16[189,128,128]{2,1,0:T(8,128)(2,1)} %param.12, bf16[128,189,128]{2,1,0:T(8,128)(2,1)} %broadcast_select_fusion), kind=kOutput, calls=%fused_computation.10 | convolution fusion | flops 826310656 | bytes 13238272 | tf_op jit(solution)/shard_map/dot_general | solution.py:18
  243.0 0.9 reshape.100
  (10 shorter events, 0.2 us)
Async XLA Ops:
  0.0 2.8 %copy-start = (bf16[8,128,128]{2,1,0:T(8,128)(2,1)S(1)}, bf16[8,128,128]{2,1,0:T(8,128)(2,1)}, u32[]{:S(2)}) copy-start(bf16[8,128,128]{2,1,0:T(8,128)(2,1)} %param.10) | copy-start | bytes 786436
  5.3 164.8 %all-to-all-start = ((bf16[96,4,128]{2,1,0:T(4,128)(2,1)}), bf16[96,4,128]{2,1,0:T(4,128)(2,1)S(1)}, u32[]{:S(2)}, u32[]{:S(2)}) async-start(bf16[96,4,128]{2,1,0:T(4,128)(2,1)} %broadcast_select_fusion.2), calls=%async_computation | async-start | bytes 196608 | tf_op jit(solution)/shard_map/all_to_all | solution.py:43
where the time goes:
time: 245 us; the launch traced here: 244 us
  blocking collectives  115 us (47%)
  local copies, waits for them, and re-layouts  74.6 us (30%)
  starting transfers between devices  22.6 us (9%)
  matrix products  17.2 us (7%)
  other arithmetic  14.1 us (6%)
    all_gather x1, blocking collectives, body(): lax.all_gather(poles_three, ('grp', 'sub'), axis=0, tiled=True)  88.6 us
    gather x6, local copies, waits for them, and re-layouts, far_sum(): picked = source_rows[jnp.maximum(lookup, 0)]  68.9 us
    all_to_all x1, starting transfers between devices, body(): lax.all_to_all(packed, 'grp', split_axis=0, concat_axis=0, tiled=True)  22.6 us
    dot_general x3, matrix products, descend(): jnp.dot(parent, spread, preferred_element_type=jnp.float32)  16.6 us
    all_gather x1, blocking collectives, body(): lax.all_gather(poles_four, 'sub', axis=0, tiled=True)  13.9 us
    all_gather x1, blocking collectives, body(): lax.all_gather(poles_five, 'sub', axis=0, tiled=True)  12.9 us
    select_n x3, other arithmetic, far_sum(): jnp.where((lookup >= 0)[:, :, None], picked, jnp.zeros((), source_rows.dt...  7.15 us
  transfers between devices with their start and end apart: 1, of which 0 were waited for; matrix products, arithmetic and copies ran while one was open for 11% of the time, Pallas kernels for 0%

commit v1 on v0

v1 whole, which is shorter than its diff:
```python
import functools

import jax
import jax.numpy as jnp
from jax import lax
from jax.experimental import pallas as pl
from jax.experimental.pallas import tpu as pltpu
from jax.sharding import PartitionSpec as P

K = 128
CLASSES = 189
CAP = 4
GROUPS = 96
SUBS = 8
SECT = GROUPS // SUBS
NEAR = 1024
EMPTY = 1535
STEP = 9
STEPS = CLASSES // STEP
MESH = pl.DeviceIdType.MESH
F32 = jnp.float32
BF16 = jnp.bfloat16


def mm(a, b):
    return jnp.dot(a, b, preferred_element_type=F32)


def ascend(rows, count, wide, up):
    wide[pl.ds(0, 8 * count), :] = rows.astype(F32)
    total = jnp.zeros((count, K), F32)
    for c in range(8):
        total += mm(wide[pl.ds(c, count, stride=8), :].astype(BF16), up[c])
    return total.astype(BF16)


def column(block, c):
    return jnp.take_along_axis(block, jnp.full(block.shape, c, jnp.int32), axis=1)


def kernel(
    mult, up, down, src5, src4, src3, boxes, counts, ops_hbm, out,
    five, pack32, pack, slots, store, tops, ops, hot5, hot3, idx5, idx4, idx3, tmp, wide, picks3,
    ops_sem, five_send, five_recv, slot_send, slot_recv, top_send, top_recv, rest_send, rest_recv,
):
    g = lax.axis_index("grp")
    s = lax.axis_index("sub")
    gs = lax.rem(g, SUBS)
    twin = gs == s

    fetch = pltpu.make_async_copy(ops_hbm, ops, ops_sem)
    fetch.start()

    barrier = pltpu.get_barrier_semaphore()

    def greet(i, carry):
        pl.semaphore_signal(barrier, inc=1, device_id=(lax.rem(g + i, GROUPS), s), device_id_type=MESH)
        return carry

    for i in range(1, SUBS):
        pl.semaphore_signal(barrier, inc=1, device_id=(g, lax.rem(s + i, SUBS)), device_id_type=MESH)
    lax.fori_loop(1, GROUPS, greet, 0)

    def partner(m):
        j = s + SUBS * m
        return j, jnp.logical_not(jnp.logical_and(twin, j == g))

    def greet_tops(m, carry):
        j, other = partner(m)

        @pl.when(other)
        def _():
            pl.semaphore_signal(barrier, inc=1, device_id=(j, gs), device_id_type=MESH)

        return carry

    lax.fori_loop(0, SECT, greet_tops, 0)

    mine = ascend(mult[...], 128, wide, up)
    own = pl.multiple_of(s * 128, 128)
    five[pl.ds(own, 128), :] = mine

    box = lax.broadcasted_iota(jnp.int32, (128, GROUPS), 0)
    for k in range(CAP):
        hit = jnp.logical_and(box == boxes[k : k + 1, :], counts[...] > k)
        chosen = lax.dot_general(
            jnp.where(hit, 1.0, 0.0).astype(BF16), mine, (((0,), (0,)), ((), ())), preferred_element_type=F32
        )
        pack32[pl.ds(k, GROUPS, stride=CAP), :] = chosen
    pack[...] = pack32[...].reshape(GROUPS, CAP, K).astype(BF16)

    pl.semaphore_wait(barrier, GROUPS - 1 + SUBS - 1 + SECT - twin.astype(jnp.int32))

    def five_copy(i):
        rows = five.at[pl.ds(own, 128), :]
        return pltpu.make_async_remote_copy(
            src_ref=rows, dst_ref=rows, send_sem=five_send, recv_sem=five_recv,
            device_id=(g, lax.rem(s + i, SUBS)), device_id_type=MESH,
        )

    for i in range(1, SUBS):
        five_copy(i).start()

    slots[g] = pack[g]

    def send_slot(i, carry):
        j = lax.rem(g + i, GROUPS)
        pltpu.make_async_remote_copy(
            src_ref=pack.at[j], dst_ref=slots.at[g], send_sem=slot_send, recv_sem=slot_recv,
            device_id=(j, s), device_id_type=MESH,
        ).start()
        return carry

    lax.fori_loop(1, GROUPS, send_slot, 0)

    tmp[pl.ds(128, 128), :] = jnp.zeros((128, 128), jnp.int32)
    tmp[pl.ds(0, CLASSES), :] = jnp.where(src5[...] < 0, EMPTY, src5[...])
    idx5[0] = jnp.transpose(tmp[pl.ds(0, 128), :])
    idx5[1] = jnp.transpose(tmp[pl.ds(128, 128), :])
    idx4[0] = src4[:, 0:128]
    idx4[1, :, 0 : CLASSES - 128] = src4[:, 128:CLASSES]
    top = src3[...]
    grp3 = jnp.right_shift(top, 4)
    place = jnp.bitwise_and(grp3, 7) * (16 * SECT) + jnp.right_shift(grp3, 3) * 16 + jnp.bitwise_and(top, 15)
    place = jnp.where(top < 0, -1, place)
    tmp[...] = jnp.zeros((256, 128), jnp.int32)
    tmp[0:2, :] = place[:, 0:128]
    tmp[128:130, 0 : CLASSES - 128] = place[:, 128:CLASSES]
    idx3[0] = jnp.transpose(tmp[pl.ds(0, 128), :])
    idx3[1] = jnp.transpose(tmp[pl.ds(128, 128), :])

    lane = lax.broadcasted_iota(jnp.int32, (128, 256), 1)

    def one_hot(col):
        low = jnp.bitwise_and(col, 255)
        return jnp.where(lane == jnp.concatenate([low, low], 1), 1.0, 0.0).astype(BF16)

    def build(i, carry):
        for q in range(3):
            c = 3 * i + q
            hot5[pl.ds(pl.multiple_of(c * 128, 128), 128), :] = one_hot(column(idx5[c // 128], c % 128))
        return carry

    lax.fori_loop(0, CLASSES // 3, build, 0)
    for t in range(2):
        for h in range(2):
            hot3[pl.ds((2 * t + h) * 128, 128), :] = one_hot(column(idx3[h], t))

    def drain(buffer, count, send, recv):
        part = buffer.at[pl.ds(0, count)]
        return pltpu.make_async_remote_copy(
            src_ref=part, dst_ref=part, send_sem=send, recv_sem=recv, device_id=(g, s), device_id_type=MESH
        )

    drain(five, 7 * 128, five_send, five_recv).wait_recv()
    four = ascend(five[...], 128, wide, up)
    three = ascend(four, 16, wide, up)

    section = pl.multiple_of(s * (16 * SECT), 16)

    held = tops.at[pl.ds(SUBS * 16 * SECT, 16), :]
    tops[pl.ds(SUBS * 16 * SECT, 16), :] = three
    spot = pl.multiple_of(gs * (16 * SECT) + (g // SUBS) * 16, 16)

    @pl.when(twin)
    def _():
        tops[pl.ds(spot, 16), :] = three

    def send_top(m, carry):
        j, other = partner(m)

        @pl.when(other)
        def _():
            pltpu.make_async_remote_copy(
                src_ref=held, dst_ref=tops.at[pl.ds(spot, 16), :], send_sem=top_send, recv_sem=top_recv,
                device_id=(j, gs), device_id_type=MESH,
            ).start()

        return carry

    lax.fori_loop(0, SECT, send_top, 0)

    fetch.wait()

    lane4 = lax.broadcasted_iota(jnp.int32, (16, 128), 1)

    def near(i, total):
        base = i * STEP
        rows = pl.ds(pl.multiple_of(base * 128, 128), STEP * 128)
        hot = hot5[rows, :]
        r0 = mm(hot, jnp.concatenate([five[0:256, :], five[256:512, :]], 1))
        r1 = mm(hot, jnp.concatenate([five[512:768, :], five[768:1024, :]], 1))
        hot4 = []
        for q in range(STEP):
            c = base + q
            hot4.append(jnp.where(lane4 == column(idx4[c // 128], c % 128), 1.0, 0.0))
        r4 = mm(jnp.concatenate(hot4, 0).astype(BF16), four)
        parts = []
        for q in range(STEP):
            c = base + q
            col = column(idx5[c // 128], c % 128)
            odd = jnp.bitwise_and(col, 256) != 0
            upper = jnp.bitwise_and(col, 512) != 0
            a = r0[q * 128 : (q + 1) * 128]
            b = r1[q * 128 : (q + 1) * 128]
            picked = jnp.where(
                upper, jnp.where(odd, b[:, 128:], b[:, :128]), jnp.where(odd, a[:, 128:], a[:, :128])
            )
            picked = jnp.where(col < NEAR, picked, 0.0)
            parts.append(jnp.concatenate([picked, r4[q * 16 : (q + 1) * 16]], 0).astype(BF16))
        weights = ops[pl.ds(base, STEP)].reshape(STEP * 128, K)
        return total + mm(jnp.concatenate(parts, 1), weights)

    half = STEPS // 3
    total = lax.fori_loop(0, half, near, jnp.zeros((144, K), F32))

    @pl.when(twin)
    def _():
        drain(tops, 16 * (SECT - 1), top_send, top_recv).wait_recv()

    @pl.when(jnp.logical_not(twin))
    def _():
        drain(tops, 16 * SECT, top_send, top_recv).wait_recv()

    for i in range(1, SUBS):
        rows = tops.at[pl.ds(section, 16 * SECT), :]
        pltpu.make_async_remote_copy(
            src_ref=rows, dst_ref=rows, send_sem=rest_send, recv_sem=rest_recv,
            device_id=(g, lax.rem(s + i, SUBS)), device_id_type=MESH,
        ).start()

    total = lax.fori_loop(half, STEPS, near, total)

    drain(tops, 7 * 16 * SECT, rest_send, rest_recv).wait_recv()
    drain(slots, GROUPS - 1, slot_send, slot_recv).wait_recv()
    store[0 : GROUPS * CAP, :] = slots[...].astype(F32).reshape(GROUPS * CAP, K).astype(BF16)
    store[GROUPS * CAP : 512, :] = jnp.zeros((512 - GROUPS * CAP, K), BF16)

    picks3[...] = jnp.zeros((2048, K), F32)
    quads = [
        mm(hot3[...], jnp.concatenate([tops[512 * b : 512 * b + 256, :], tops[512 * b + 256 : 512 * b + 512, :]], 1))
        for b in range(3)
    ]
    for t in range(2):
        for h in range(2):
            col = column(idx3[h], t)
            odd = jnp.bitwise_and(col, 256) != 0
            r = [x[(2 * t + h) * 128 : (2 * t + h + 1) * 128] for x in quads]
            r = [jnp.where(odd, x[:, 128:], x[:, :128]) for x in r]
            got = jnp.where(col >= 1024, r[2], jnp.where(col >= 512, r[1], r[0]))
            picks3[pl.ds(1024 * h + t, 128, stride=8), :] = jnp.where(col < 0, 0.0, got)

    def far(i, total):
        base = i * STEP
        rows = pl.ds(pl.multiple_of(base * 128, 128), STEP * 128)
        r = mm(hot5[rows, :], jnp.concatenate([store[0:256, :], store[256:512, :]], 1))
        parts = []
        for q in range(STEP):
            c = base + q
            col = column(idx5[c // 128], c % 128)
            odd = jnp.bitwise_and(col, 256) != 0
            a = r[q * 128 : (q + 1) * 128]
            picked = jnp.where(col < NEAR, 0.0, jnp.where(odd, a[:, 128:], a[:, :128]))
            third = picks3[pl.ds(pl.multiple_of(c * 8, 8), 8), :]
            parts.append(jnp.concatenate([picked, third], 0).astype(BF16))
        weights = ops[pl.ds(base, STEP)].reshape(STEP * 128, K)
        return total + mm(jnp.concatenate(parts, 1), weights)

    rest = lax.fori_loop(0, STEPS, far, jnp.zeros((136, K), F32))

    local = rest[128:136].astype(BF16)
    for c in range(8):
        wide[pl.ds(c, 8, stride=8), :] = mm(local, down[c])
    local = (wide[0:16, :] + total[128:144]).astype(BF16)
    for c in range(8):
        wide[pl.ds(c, 16, stride=8), :] = mm(local, down[c])
    local = (wide[0:128, :] + (total[0:128] + rest[0:128])).astype(BF16)
    for c in range(8):
        out[pl.ds(c, 128, stride=8), :] = mm(local, down[c])

    for i in range(1, SUBS):
        five_copy(i).wait_send()
    drain(slots, GROUPS - 1, slot_send, slot_recv).wait_send()

    @pl.when(twin)
    def _():
        drain(tops, 16 * (SECT - 1), top_send, top_recv).wait_send()

    @pl.when(jnp.logical_not(twin))
    def _():
        drain(tops, 16 * SECT, top_send, top_recv).wait_send()

    drain(tops, 7 * 16 * SECT, rest_send, rest_recv).wait_send()


def body(multipoles, up_ops, down_ops, far_ops, sources5, sources4, sources3, send_boxes, send_counts):
    vmem = pl.BlockSpec(memory_space=pltpu.VMEM)
    dma = pltpu.SemaphoreType.DMA
    return pl.pallas_call(
        kernel,
        out_shape=jax.ShapeDtypeStruct((1024, K), F32),
        in_specs=[vmem] * 8 + [pl.BlockSpec(memory_space=pl.ANY)],
        out_specs=vmem,
        scratch_shapes=[
            pltpu.VMEM((NEAR, K), BF16),
            pltpu.VMEM((GROUPS * CAP, K), F32),
            pltpu.VMEM((GROUPS, CAP, K), BF16),
            pltpu.VMEM((GROUPS, CAP, K), BF16),
            pltpu.VMEM((512, K), BF16),
            pltpu.VMEM((SUBS * 16 * SECT + 16, K), BF16),
            pltpu.VMEM((CLASSES, K, K), BF16),
            pltpu.VMEM((CLASSES * 128, 256), BF16),
            pltpu.VMEM((512, 256), BF16),
            pltpu.VMEM((2, 128, 128), jnp.int32),
            pltpu.VMEM((2, 16, 128), jnp.int32),
            pltpu.VMEM((2, 128, 128), jnp.int32),
            pltpu.VMEM((256, 128), jnp.int32),
            pltpu.VMEM((1024, K), F32),
            pltpu.VMEM((2048, K), F32),
        ]
        + [dma] * 9,
        compiler_params=pltpu.CompilerParams(
            collective_id=0, has_side_effects=True, vmem_limit_bytes=48 * 2**20
        ),
    )(
        multipoles, up_ops, down_ops, sources5, sources4.T, sources3.T, send_boxes[0].T, send_counts, far_ops
    )


def solution(mesh):
    in_specs = (
        P(("grp", "sub"), None),
        P(),
        P(),
        P(),
        P(None, ("grp", "sub")),
        P(None, ("grp", "sub")),
        P(None, ("grp", "sub")),
        P(("grp", "sub"), None, None),
        P(("grp", "sub"), None),
    )
    out_specs = P(("grp", "sub"), None)
    return jax.shard_map(body, mesh=mesh, in_specs=in_specs, out_specs=out_specs, check_vma=False)
```

time: 245 us -> 72.2 us (0.29)
  the two profiles are of different devices: /device:TPU:1 before, /device:TPU:57 now
where the time goes in v1:
time: 72.2 us; the launch traced here: 71.8 us
  Pallas kernels  64.6 us (89%)
  local copies, waits for them, and re-layouts  7.27 us (10%)
    pallas_call x1, Pallas kernels, body(): pl.pallas_call(kernel, out_shape=jax.ShapeDtypeStruct((1024, K), F32), in...  64.6 us
    unnamed x17, local copies, waits for them, and re-layouts  7.27 us

profile of v1, /device:TPU:57, one launch (start us, length us, event | category | flops | bytes accessed | tf_op | source)
XLA Modules:
  0.0 71.8 jit_solution(3221646417891071860)
XLA Ops:
  0.0 0.0 copy-start
  0.0 0.9 %copy-done = bf16[1024,128]{1,0:T(8,128)(2,1)S(1)} copy-done((bf16[1024,128]{1,0:T(8,128)(2,1)S(1)}, bf16[1024,128]{1,0:T(8,128)(2,1)}, u32[]{:S(2)}) %copy-start) | copy-done | bytes 262168
  1.0 0.0 copy-start.1
  1.0 0.9 %copy-done.1 = bf16[8,128,128]{2,1,0:T(8,128)(2,1)S(1)} copy-done((bf16[8,128,128]{2,1,0:T(8,128)(2,1)S(1)}, bf16[8,128,128]{2,1,0:T(8,128)(2,1)}, u32[]{:S(2)}) %copy-start.1) | copy-done | bytes 262168
  1.9 0.0 copy-start.2
  1.9 0.9 %copy-done.2 = bf16[8,128,128]{2,1,0:T(8,128)(2,1)S(1)} copy-done((bf16[8,128,128]{2,1,0:T(8,128)(2,1)S(1)}, bf16[8,128,128]{2,1,0:T(8,128)(2,1)}, u32[]{:S(2)}) %copy-start.2) | copy-done | bytes 262168
  2.9 0.0 copy-start.3
  2.9 0.9 %copy-done.3 = s32[189,128]{1,0:T(8,128)S(1)} copy-done((s32[189,128]{1,0:T(8,128)S(1)}, s32[189,128]{1,0:T(8,128)}, u32[]{:S(2)}) %copy-start.3) | copy-done | bytes 96792
  3.7 0.0 copy-start.4
  3.7 0.7 copy-done.4
  4.5 0.0 copy-start.5
  4.5 0.7 copy-done.5
  5.1 0.0 copy-start.6
  5.1 0.7 copy-done.6
  5.8 0.0 copy-start.7
  5.8 0.7 copy-done.7
  6.5 64.6 %shard_map.91 = f32[1024,128]{1,0:T(8,128)S(1)} custom-call(bf16[1024,128]{1,0:T(8,128)(2,1)S(1)} %copy-done, bf16[8,128,128]{2,1,0:T(8,128)(2,1)S(1)} %copy-done.1, bf16[8,128,128]{2,1,0:T(8,128)(2,1)S(1)} %copy-done.2, s32[189,128]{1,0:T(8,128)S(1)} %copy-done.3, s32[16,189]{1,0:T(8,128)S(1)} %bitcast.5, s32[2,189]{1,0:T(2,128)S(1)} %bitcast.6, ...), custom_call_target="tpu_custom_call" | custom-call | tf_op jit(solution)/shard_map/pallas_call | solution.py:299
  71.1 0.8 %copy.11 = f32[1024,128]{1,0:T(8,128)} copy(f32[1024,128]{1,0:T(8,128)S(1)} %shard_map.91) | data formatting | bytes 1048576
Async XLA Ops:
  0.0 0.9 %copy-start = (bf16[1024,128]{1,0:T(8,128)(2,1)S(1)}, bf16[1024,128]{1,0:T(8,128)(2,1)}, u32[]{:S(2)}) copy-start(bf16[1024,128]{1,0:T(8,128)(2,1)} %mult.1) | copy-start | bytes 786436
  1.0 0.9 %copy-start.1 = (bf16[8,128,128]{2,1,0:T(8,128)(2,1)S(1)}, bf16[8,128,128]{2,1,0:T(8,128)(2,1)}, u32[]{:S(2)}) copy-start(bf16[8,128,128]{2,1,0:T(8,128)(2,1)} %up.1) | copy-start | bytes 786436
  1.9 0.9 %copy-start.2 = (bf16[8,128,128]{2,1,0:T(8,128)(2,1)S(1)}, bf16[8,128,128]{2,1,0:T(8,128)(2,1)}, u32[]{:S(2)}) copy-start(bf16[8,128,128]{2,1,0:T(8,128)(2,1)} %down.1) | copy-start | bytes 786436
  2.9 0.9 %copy-start.3 = (s32[189,128]{1,0:T(8,128)S(1)}, s32[189,128]{1,0:T(8,128)}, u32[]{:S(2)}) copy-start(s32[189,128]{1,0:T(8,128)} %src5.1) | copy-start | bytes 290308
  3.7 0.7 copy-start.4
  4.5 0.7 copy-start.5
  5.1 0.7 copy-start.6
  5.8 0.7 copy-start.7

commit v2 on v1

v2 whole, which is shorter than its diff:
```python
import functools

import jax
import jax.numpy as jnp
from jax import lax
from jax.experimental import pallas as pl
from jax.experimental.pallas import tpu as pltpu
from jax.sharding import PartitionSpec as P

K = 128
CLASSES = 189
CAP = 4
GROUPS = 96
SUBS = 8
SIDE = 8
RING = GROUPS // SIDE
MESSAGE = 8
SECT = 2 * GROUPS
NEAR = 1024
EMPTY = 1535
STEP = 63
BUILD = 63
STEPS = CLASSES // STEP
MESH = pl.DeviceIdType.MESH
F32 = jnp.float32
BF16 = jnp.bfloat16


def mm(a, b):
    return jnp.dot(a, b, preferred_element_type=F32)


def ascend(rows, count, wide, up):
    wide[pl.ds(0, 8 * count), :] = rows.astype(F32)
    total = jnp.zeros((count, K), F32)
    for c in range(8):
        total += mm(wide[pl.ds(c, count, stride=8), :].astype(BF16), up[c])
    return total.astype(BF16)


def column(block, c):
    return jnp.take_along_axis(block, jnp.full(block.shape, c, jnp.int32), axis=1)


def kernel(
    mult_hbm, up_hbm, down_hbm, src5_hbm, src4_hbm, src3_hbm, boxes_hbm, counts_hbm, ops_hbm, out,
    mult, up, down, src5, src4, src3, boxes, counts, ops,
    five, pack32, pack, slots, store, tops, hot5, hot3, picks0, picks1, picks2, picks43, idx5, low5, idx4, idx3, tmp, wide, picks3,
    in_sems, five_send, five_recv, slot_send, slot_recv, rest_send, rest_recv,
):
    g = lax.axis_index("grp")
    s = lax.axis_index("sub")

    loads = [
        pltpu.make_async_copy(src, dst, in_sems.at[i])
        for i, (src, dst) in enumerate(
            [
                (mult_hbm, mult), (up_hbm, up), (boxes_hbm, boxes), (counts_hbm, counts), (src5_hbm, src5),
                (src4_hbm, src4), (src3_hbm, src3), (down_hbm, down), (ops_hbm, ops),
            ]
        )
    ]
    for load in loads:
        load.start()

    barrier = pltpu.get_barrier_semaphore()

    def peer(i):
        kz = i // SIDE
        ky = lax.rem(i, SIDE)
        dz = RING // 2 + ((kz + 1) // 2) * (1 - 2 * lax.rem(kz, 2))
        dy = SIDE // 2 + ((ky + 1) // 2) * (1 - 2 * lax.rem(ky, 2))
        return lax.rem(g // RING + dy, SIDE) * RING + lax.rem(lax.rem(g, RING) + dz, RING)

    def greet(i, carry):
        pl.semaphore_signal(barrier, inc=1, device_id=(peer(i), s), device_id_type=MESH)
        return carry

    lax.fori_loop(0, GROUPS - 1, greet, 0)
    for i in range(1, SUBS):
        pl.semaphore_signal(barrier, inc=1, device_id=(g, lax.rem(s + i, SUBS)), device_id_type=MESH)

    loads[0].wait()
    loads[1].wait()
    mine = ascend(mult[...], 128, wide, up)
    own = pl.multiple_of(s * 128, 128)
    five[pl.ds(own, 128), :] = mine
    top = ascend(ascend(mine, 16, wide, up), 2, wide, up).astype(F32)

    loads[2].wait()
    loads[3].wait()
    box = lax.broadcasted_iota(jnp.int32, (128, GROUPS), 0)
    for k in range(CAP):
        hit = jnp.logical_and(box == boxes[k : k + 1, :], counts[...] > k)
        pack32[pl.ds(k, GROUPS, stride=MESSAGE), :] = lax.dot_general(
            jnp.where(hit, 1.0, 0.0).astype(BF16), mine, (((0,), (0,)), ((), ())), preferred_element_type=F32
        )
    for r in range(2):
        pack32[pl.ds(CAP + r, GROUPS, stride=MESSAGE), :] = jnp.broadcast_to(top[r : r + 1], (GROUPS, K))
        pack32[pl.ds(CAP + 2 + r, GROUPS, stride=MESSAGE), :] = jnp.zeros((GROUPS, K), F32)
    pack[...] = pack32[...].reshape(GROUPS, MESSAGE, K).astype(BF16)

    pl.semaphore_wait(barrier, GROUPS - 1 + SUBS - 1)

    def round_group(rows, send, recv):
        return [
            pltpu.make_async_remote_copy(
                src_ref=rows, dst_ref=rows, send_sem=send, recv_sem=recv,
                device_id=(g, lax.rem(s + i, SUBS)), device_id_type=MESH,
            )
            for i in range(1, SUBS)
        ]

    def drain(buffer, count, send, recv):
        part = buffer.at[pl.ds(0, count)]
        return pltpu.make_async_remote_copy(
            src_ref=part, dst_ref=part, send_sem=send, recv_sem=recv, device_id=(g, s), device_id_type=MESH
        )

    for copy in round_group(five.at[pl.ds(own, 128), :], five_send, five_recv):
        copy.start()

    slots[g] = pack[g]

    def send_slot(i, carry):
        j = peer(i)
        pltpu.make_async_remote_copy(
            src_ref=pack.at[j], dst_ref=slots.at[g], send_sem=slot_send, recv_sem=slot_recv,
            device_id=(j, s), device_id_type=MESH,
        ).start()
        return carry

    lax.fori_loop(0, GROUPS - 1, send_slot, 0)

    for load in loads[4:7]:
        load.wait()
    tmp[pl.ds(128, 128), :] = jnp.zeros((128, 128), jnp.int32)
    entry = src5[...]
    slot = entry - NEAR
    slot = NEAR + jnp.bitwise_and(slot, 3) * GROUPS + jnp.right_shift(slot, 2)
    tmp[pl.ds(0, CLASSES), :] = jnp.where(entry < 0, EMPTY, jnp.where(entry < NEAR, entry, slot))
    idx5[0] = jnp.transpose(tmp[pl.ds(0, 128), :])
    idx5[1] = jnp.transpose(tmp[pl.ds(128, 128), :])
    low5[...] = jnp.bitwise_and(idx5[...], 255)
    idx5[...] = jnp.right_shift(idx5[...], 8)
    idx4[0] = src4[:, 0:128]
    idx4[1, :, 0 : CLASSES - 128] = src4[:, 128:CLASSES]
    entry = src3[...]
    place = jnp.bitwise_and(jnp.right_shift(entry, 1), 7) * SECT + jnp.bitwise_and(entry, 1) * GROUPS
    place = jnp.where(entry < 0, -1, place + jnp.right_shift(entry, 4))
    tmp[...] = jnp.zeros((256, 128), jnp.int32)
    tmp[0:2, :] = place[:, 0:128]
    tmp[128:130, 0 : CLASSES - 128] = place[:, 128:CLASSES]
    idx3[0] = jnp.transpose(tmp[pl.ds(0, 128), :])
    idx3[1] = jnp.transpose(tmp[pl.ds(128, 128), :])

    lane = lax.broadcasted_iota(jnp.int32, (128, 256), 1)

    def one_hot(low):
        return jnp.where(lane == jnp.concatenate([low, low], 1), 1.0, 0.0).astype(BF16)

    def build(i, carry):
        for q in range(BUILD):
            c = BUILD * i + q
            hot5[pl.ds(pl.multiple_of(c * 128, 128), 128), :] = one_hot(column(low5[c // 128], c % 128))
        return carry

    lax.fori_loop(0, CLASSES // BUILD, build, 0)
    for t in range(2):
        for h in range(2):
            hot3[pl.ds((2 * t + h) * 128, 128), :] = one_hot(jnp.bitwise_and(column(idx3[h], t), 255))
    picks3[...] = jnp.zeros((2048, K), F32)

    drain(five, 7 * 128, five_send, five_recv).wait_recv()
    four = ascend(five[...], 128, wide, up)
    lane4 = lax.broadcasted_iota(jnp.int32, (16, 128), 1)

    def lanes(c):
        return pl.ds(pl.multiple_of(c * K, K), K)

    def tiles(c, *parts):
        hot = hot5[pl.ds(pl.multiple_of(c * 128, 128), 128), :]
        block = column(idx5[c // 128], c % 128)
        for b, table, picks in parts:
            r = mm(hot, table)
            picked = jnp.where(block == 2 * b, r[:, :K], jnp.where(block == 2 * b + 1, r[:, K:], 0.0))
            picks[:, lanes(c)] = picked.astype(BF16)

    def near(i, carry):
        first = jnp.concatenate([five[0:256, :], five[256:512, :]], 1)
        second = jnp.concatenate([five[512:768, :], five[768:1024, :]], 1)
        base = i * STEP
        hot4 = []
        for q in range(STEP):
            c = base + q
            tiles(c, (0, first, picks0), (1, second, picks1))
            hot4.append(jnp.where(lane4 == column(idx4[c // 128], c % 128), 1.0, 0.0))
        r4 = mm(jnp.concatenate(hot4, 0).astype(BF16), four)
        for q in range(STEP):
            picks43[0:16, lanes(base + q)] = r4[q * 16 : (q + 1) * 16].astype(BF16)
        return carry

    early = CLASSES // STEP - 1
    lax.fori_loop(0, early, near, 0)

    drain(slots, GROUPS - 1, slot_send, slot_recv).wait_recv()
    wide[0 : GROUPS * MESSAGE, :] = slots[...].astype(F32).reshape(GROUPS * MESSAGE, K)
    for k in range(CAP):
        store[k * GROUPS : (k + 1) * GROUPS, :] = wide[pl.ds(k, GROUPS, stride=MESSAGE), :].astype(BF16)
    store[GROUPS * CAP : 512, :] = jnp.zeros((512 - GROUPS * CAP, K), BF16)
    section = pl.multiple_of(s * SECT, SECT)
    for r in range(2):
        tops[pl.ds(pl.multiple_of(section + r * GROUPS, GROUPS), GROUPS), :] = wide[
            pl.ds(CAP + r, GROUPS, stride=MESSAGE), :
        ].astype(BF16)
    for copy in round_group(tops.at[pl.ds(section, SECT), :], rest_send, rest_recv):
        copy.start()

    lax.fori_loop(early, CLASSES // STEP, near, 0)

    def far(i, carry):
        third = jnp.concatenate([store[0:256, :], store[256:512, :]], 1)
        for q in range(STEP):
            tiles(i * STEP + q, (2, third, picks2))
        return carry

    lax.fori_loop(0, CLASSES // STEP, far, 0)

    drain(tops, 7 * SECT, rest_send, rest_recv).wait_recv()
    quads = [
        mm(hot3[...], jnp.concatenate([tops[512 * b : 512 * b + 256, :], tops[512 * b + 256 : 512 * b + 512, :]], 1))
        for b in range(3)
    ]
    for t in range(2):
        for h in range(2):
            col = column(idx3[h], t)
            odd = jnp.bitwise_and(col, 256) != 0
            r = [x[(2 * t + h) * 128 : (2 * t + h + 1) * 128] for x in quads]
            r = [jnp.where(odd, x[:, 128:], x[:, :128]) for x in r]
            got = jnp.where(col >= 1024, r[2], jnp.where(col >= 512, r[1], r[0]))
            picks3[pl.ds(1024 * h + t, 128, stride=8), :] = jnp.where(col < 0, 0.0, got)

    loads[8].wait()

    def apply(i, total):
        base = i * STEP
        for q in range(STEP):
            c = base + q
            rows = picks3[pl.ds(pl.multiple_of(c * 8, 8), 8), :]
            picks43[16:32, lanes(c)] = jnp.concatenate([rows, rows], 0).astype(BF16)
        span = pl.ds(pl.multiple_of(base * K, K), STEP * K)
        picked = jnp.concatenate([picks0[:, span] + picks1[:, span] + picks2[:, span], picks43[:, span]], 0)
        return total + mm(picked, ops[pl.ds(base, STEP)].reshape(STEP * K, K))

    total = lax.fori_loop(0, CLASSES // STEP, apply, jnp.zeros((160, K), F32))

    loads[7].wait()
    local = total[144:152].astype(BF16)
    for c in range(8):
        wide[pl.ds(c, 8, stride=8), :] = mm(local, down[c])
    local = (wide[0:16, :] + total[128:144]).astype(BF16)
    for c in range(8):
        wide[pl.ds(c, 16, stride=8), :] = mm(local, down[c])
    local = (wide[0:128, :] + total[0:128]).astype(BF16)
    for c in range(8):
        out[pl.ds(c, 128, stride=8), :] = mm(local, down[c])

    drain(five, 7 * 128, five_send, five_recv).wait_send()
    drain(slots, GROUPS - 1, slot_send, slot_recv).wait_send()
    drain(tops, 7 * SECT, rest_send, rest_recv).wait_send()


def body(multipoles, up_ops, down_ops, far_ops, sources5, sources4, sources3, send_boxes, send_counts):
    dma = pltpu.SemaphoreType.DMA
    operands = (
        multipoles, up_ops, down_ops, sources5, sources4.T, sources3.T, send_boxes[0].T, send_counts, far_ops
    )
    return pl.pallas_call(
        kernel,
        out_shape=jax.ShapeDtypeStruct((1024, K), F32),
        in_specs=[pl.BlockSpec(memory_space=pl.ANY)] * 9,
        out_specs=pl.BlockSpec(memory_space=pltpu.VMEM),
        scratch_shapes=[pltpu.VMEM(x.shape, x.dtype) for x in operands]
        + [
            pltpu.VMEM((NEAR, K), BF16),
            pltpu.VMEM((GROUPS * MESSAGE, K), F32),
            pltpu.VMEM((GROUPS, MESSAGE, K), BF16),
            pltpu.VMEM((GROUPS, MESSAGE, K), BF16),
            pltpu.VMEM((512, K), BF16),
            pltpu.VMEM((SUBS * SECT, K), BF16),
            pltpu.VMEM((CLASSES * 128, 256), BF16),
            pltpu.VMEM((512, 256), BF16),
            pltpu.VMEM((128, CLASSES * K), BF16),
            pltpu.VMEM((128, CLASSES * K), BF16),
            pltpu.VMEM((128, CLASSES * K), BF16),
            pltpu.VMEM((32, CLASSES * K), BF16),
            pltpu.VMEM((2, 128, 128), jnp.int32),
            pltpu.VMEM((2, 128, 128), jnp.int32),
            pltpu.VMEM((2, 16, 128), jnp.int32),
            pltpu.VMEM((2, 128, 128), jnp.int32),
            pltpu.VMEM((256, 128), jnp.int32),
            pltpu.VMEM((1024, K), F32),
            pltpu.VMEM((2048, K), F32),
            dma((9,)),
        ]
        + [dma] * 6,
        compiler_params=pltpu.CompilerParams(
            collective_id=0, has_side_effects=True, vmem_limit_bytes=56 * 2**20
        ),
    )(*operands)


def solution(mesh):
    in_specs = (
        P(("grp", "sub"), None),
        P(),
        P(),
        P(),
        P(None, ("grp", "sub")),
        P(None, ("grp", "sub")),
        P(None, ("grp", "sub")),
        P(("grp", "sub"), None, None),
        P(("grp", "sub"), None),
    )
    out_specs = P(("grp", "sub"), None)
    return jax.shard_map(body, mesh=mesh, in_specs=in_specs, out_specs=out_specs, check_vma=False)
```

time: 72.2 us -> 50.1 us (0.69)
  the two profiles are of different devices: /device:TPU:57 before, /device:TPU:1 now
where the time goes in v2:
time: 50.1 us; the launch traced here: 49.9 us
  Pallas kernels  48 us (96%)
  local copies, waits for them, and re-layouts  1.87 us (4%)
    pallas_call x1, Pallas kernels, body(): pl.pallas_call(kernel, out_shape=jax.ShapeDtypeStruct((1024, K), F32), in...  48 us
    unnamed x1, local copies, waits for them, and re-layouts  1.87 us

profile of v2, /device:TPU:1, one launch (start us, length us, event | category | flops | bytes accessed | tf_op | source)
XLA Modules:
  0.0 49.9 jit_solution(2437948345741855704)
XLA Ops:
  0.0 48.0 %shard_map.91 = f32[1024,128]{1,0:T(8,128)} custom-call(bf16[1024,128]{1,0:T(8,128)(2,1)} %mult_hbm.1, bf16[8,128,128]{2,1,0:T(8,128)(2,1)} %up_hbm.1, bf16[8,128,128]{2,1,0:T(8,128)(2,1)} %down_hbm.1, s32[189,128]{1,0:T(8,128)} %src5_hbm.1, s32[16,189]{1,0:T(8,128)} %bitcast.5, s32[2,189]{1,0:T(2,128)} %bitcast.6, s32[4,96]{1,0:T(4,128)} %bitcast.7, ...), custom_call_target="tpu_custom_call" | custom-call | tf_op jit(solution)/shard_map/pallas_call | solution.py:278
  48.0 1.9 %copy.11 = f32[1024,128]{1,0:T(8,128)} copy(f32[1024,128]{1,0:T(8,128)} %shard_map.91) | data formatting | bytes 1048576

commit v3 on v2

--- a/solution.py
+++ b/solution.py
@@ -99,38 +99,6 @@
         pack32[pl.ds(CAP + r, GROUPS, stride=MESSAGE), :] = jnp.broadcast_to(top[r : r + 1], (GROUPS, K))
         pack32[pl.ds(CAP + 2 + r, GROUPS, stride=MESSAGE), :] = jnp.zeros((GROUPS, K), F32)
     pack[...] = pack32[...].reshape(GROUPS, MESSAGE, K).astype(BF16)
-
-    pl.semaphore_wait(barrier, GROUPS - 1 + SUBS - 1)
-
-    def round_group(rows, send, recv):
-        return [
-            pltpu.make_async_remote_copy(
-                src_ref=rows, dst_ref=rows, send_sem=send, recv_sem=recv,
-                device_id=(g, lax.rem(s + i, SUBS)), device_id_type=MESH,
-            )
-            for i in range(1, SUBS)
-        ]
-
-    def drain(buffer, count, send, recv):
-        part = buffer.at[pl.ds(0, count)]
-        return pltpu.make_async_remote_copy(
-            src_ref=part, dst_ref=part, send_sem=send, recv_sem=recv, device_id=(g, s), device_id_type=MESH
-        )
-
-    for copy in round_group(five.at[pl.ds(own, 128), :], five_send, five_recv):
-        copy.start()
-
-    slots[g] = pack[g]
-
-    def send_slot(i, carry):
-        j = peer(i)
-        pltpu.make_async_remote_copy(
-            src_ref=pack.at[j], dst_ref=slots.at[g], send_sem=slot_send, recv_sem=slot_recv,
-            device_id=(j, s), device_id_type=MESH,
-        ).start()
-        return carry
-
-    lax.fori_loop(0, GROUPS - 1, send_slot, 0)
 
     for load in loads[4:7]:
         load.wait()
@@ -170,6 +138,38 @@
         for h in range(2):
             hot3[pl.ds((2 * t + h) * 128, 128), :] = one_hot(jnp.bitwise_and(column(idx3[h], t), 255))
     picks3[...] = jnp.zeros((2048, K), F32)
+
+    pl.semaphore_wait(barrier, GROUPS - 1 + SUBS - 1)
+
+    def round_group(rows, send, recv):
+        return [
+            pltpu.make_async_remote_copy(
+                src_ref=rows, dst_ref=rows, send_sem=send, recv_sem=recv,
+                device_id=(g, lax.rem(s + i, SUBS)), device_id_type=MESH,
+            )
+            for i in range(1, SUBS)
+        ]
+
+    def drain(buffer, count, send, recv):
+        part = buffer.at[pl.ds(0, count)]
+        return pltpu.make_async_remote_copy(
+            src_ref=part, dst_ref=part, send_sem=send, recv_sem=recv, device_id=(g, s), device_id_type=MESH
+        )
+
+    for copy in round_group(five.at[pl.ds(own, 128), :], five_send, five_recv):
+        copy.start()
+
+    slots[g] = pack[g]
+
+    def send_slot(i, carry):
+        j = peer(i)
+        pltpu.make_async_remote_copy(
+            src_ref=pack.at[j], dst_ref=slots.at[g], send_sem=slot_send, recv_sem=slot_recv,
+            device_id=(j, s), device_id_type=MESH,
+        ).start()
+        return carry
+
+    lax.fori_loop(0, GROUPS - 1, send_slot, 0)
 
     drain(five, 7 * 128, five_send, five_recv).wait_recv()
     four = ascend(five[...], 128, wide, up)
@@ -305,7 +305,7 @@
         ]
         + [dma] * 6,
         compiler_params=pltpu.CompilerParams(
-            collective_id=0, has_side_effects=True, vmem_limit_bytes=56 * 2**20
+            collective_id=0, has_side_effects=True, vmem_limit_bytes=46 * 2**20
         ),
     )(*operands)
 

time: 50.1 us -> 58.8 us (1.17)
  local copies, waits for them, and re-layouts: 1.87 us -> 10 us
    unnamed x1 -> x19, local copies, waits for them, and re-layouts: 1.87 us -> 10 us
where the time goes in v3:
time: 58.8 us; the launch traced here: 58.4 us
  Pallas kernels  48.4 us (82%)
  local copies, waits for them, and re-layouts  10 us (17%)
    pallas_call x1, Pallas kernels, body(): pl.pallas_call(kernel, out_shape=jax.ShapeDtypeStruct((1024, K), F32), in...  48.4 us
    unnamed x19, local copies, waits for them, and re-layouts  10 us

profile of v3, /device:TPU:1, one launch (start us, length us, event | category | flops | bytes accessed | tf_op | source)
XLA Modules:
  0.0 58.4 jit_solution(4050411037676236915)
XLA Ops:
  0.0 0.0 copy-start
  0.0 2.8 %copy-done = bf16[189,128,128]{2,1,0:T(8,128)(2,1)S(1)} copy-done((bf16[189,128,128]{2,1,0:T(8,128)(2,1)S(1)}, bf16[189,128,128]{2,1,0:T(8,128)(2,1)}, u32[]{:S(2)}) %copy-start) | copy-done | bytes 6193176
  2.8 0.0 copy-start.1
  2.8 0.9 %copy-done.1 = bf16[1024,128]{1,0:T(8,128)(2,1)S(1)} copy-done((bf16[1024,128]{1,0:T(8,128)(2,1)S(1)}, bf16[1024,128]{1,0:T(8,128)(2,1)}, u32[]{:S(2)}) %copy-start.1) | copy-done | bytes 262168
  3.7 0.0 copy-start.2
  3.7 0.9 %copy-done.2 = bf16[8,128,128]{2,1,0:T(8,128)(2,1)S(1)} copy-done((bf16[8,128,128]{2,1,0:T(8,128)(2,1)S(1)}, bf16[8,128,128]{2,1,0:T(8,128)(2,1)}, u32[]{:S(2)}) %copy-start.2) | copy-done | bytes 262168
  4.7 0.0 copy-start.3
  4.7 0.9 %copy-done.3 = bf16[8,128,128]{2,1,0:T(8,128)(2,1)S(1)} copy-done((bf16[8,128,128]{2,1,0:T(8,128)(2,1)S(1)}, bf16[8,128,128]{2,1,0:T(8,128)(2,1)}, u32[]{:S(2)}) %copy-start.3) | copy-done | bytes 262168
  5.6 0.0 copy-start.4
  5.6 0.9 %copy-done.4 = s32[189,128]{1,0:T(8,128)S(1)} copy-done((s32[189,128]{1,0:T(8,128)S(1)}, s32[189,128]{1,0:T(8,128)}, u32[]{:S(2)}) %copy-start.4) | copy-done | bytes 96792
  6.5 0.0 copy-start.5
  6.5 0.7 %copy-done.5 = s32[189,16]{0,1:T(8,128)S(1)} copy-done((s32[189,16]{0,1:T(8,128)S(1)}, s32[189,16]{0,1:T(8,128)}, u32[]{:S(2)}) %copy-start.5) | copy-done | bytes 12120
  7.2 0.0 copy-start.6
  7.2 0.7 %copy-done.6 = s32[189,2]{0,1:T(2,128)S(1)} copy-done((s32[189,2]{0,1:T(2,128)S(1)}, s32[189,2]{0,1:T(2,128)}, u32[]{:S(2)}) %copy-start.6) | copy-done | bytes 1536
  7.9 0.0 copy-start.7
  7.9 0.7 %copy-done.7 = s32[1,96,4]{1,2,0:T(4,128)S(1)} copy-done((s32[1,96,4]{1,2,0:T(4,128)S(1)}, s32[1,96,4]{1,2,0:T(4,128)}, u32[]{:S(2)}) %copy-start.7) | copy-done | bytes 1560
  8.6 0.0 copy-start.8
  8.6 0.7 %copy-done.8 = s32[1,96]{1,0:T(1,128)S(1)} copy-done((s32[1,96]{1,0:T(1,128)S(1)}, s32[1,96]{1,0:T(1,128)}, u32[]{:S(2)}) %copy-start.8) | copy-done | bytes 408
  9.2 48.4 %shard_map.91 = f32[1024,128]{1,0:T(8,128)S(1)} custom-call(bf16[1024,128]{1,0:T(8,128)(2,1)S(1)} %copy-done.1, bf16[8,128,128]{2,1,0:T(8,128)(2,1)S(1)} %copy-done.2, bf16[8,128,128]{2,1,0:T(8,128)(2,1)S(1)} %copy-done.3, s32[189,128]{1,0:T(8,128)S(1)} %copy-done.4, s32[16,189]{1,0:T(8,128)S(1)} %bitcast.5, s32[2,189]{1,0:T(2,128)S(1)} %bitcast.6, ...), custom_call_target="tpu_custom_call" | custom-call | tf_op jit(solution)/shard_map/pallas_call | solution.py:278
  57.6 0.8 %copy.11 = f32[1024,128]{1,0:T(8,128)} copy(f32[1024,128]{1,0:T(8,128)S(1)} %shard_map.91) | data formatting | bytes 1048576
Async XLA Ops:
  0.0 2.8 %copy-start = (bf16[189,128,128]{2,1,0:T(8,128)(2,1)S(1)}, bf16[189,128,128]{2,1,0:T(8,128)(2,1)}, u32[]{:S(2)}) copy-start(bf16[189,128,128]{2,1,0:T(8,128)(2,1)} %ops_hbm.1) | copy-start | bytes 18579460
  2.8 0.9 %copy-start.1 = (bf16[1024,128]{1,0:T(8,128)(2,1)S(1)}, bf16[1024,128]{1,0:T(8,128)(2,1)}, u32[]{:S(2)}) copy-start(bf16[1024,128]{1,0:T(8,128)(2,1)} %mult_hbm.1) | copy-start | bytes 786436
  3.7 0.9 %copy-start.2 = (bf16[8,128,128]{2,1,0:T(8,128)(2,1)S(1)}, bf16[8,128,128]{2,1,0:T(8,128)(2,1)}, u32[]{:S(2)}) copy-start(bf16[8,128,128]{2,1,0:T(8,128)(2,1)} %up_hbm.1) | copy-start | bytes 786436
  4.7 0.9 %copy-start.3 = (bf16[8,128,128]{2,1,0:T(8,128)(2,1)S(1)}, bf16[8,128,128]{2,1,0:T(8,128)(2,1)}, u32[]{:S(2)}) copy-start(bf16[8,128,128]{2,1,0:T(8,128)(2,1)} %down_hbm.1) | copy-start | bytes 786436
  5.6 0.9 %copy-start.4 = (s32[189,128]{1,0:T(8,128)S(1)}, s32[189,128]{1,0:T(8,128)}, u32[]{:S(2)}) copy-start(s32[189,128]{1,0:T(8,128)} %src5_hbm.1) | copy-start | bytes 290308
  6.5 0.7 %copy-start.5 = (s32[189,16]{0,1:T(8,128)S(1)}, s32[189,16]{0,1:T(8,128)}, u32[]{:S(2)}) copy-start(s32[189,16]{0,1:T(8,128)} %param.14) | copy-start | bytes 36292
  7.2 0.7 %copy-start.6 = (s32[189,2]{0,1:T(2,128)S(1)}, s32[189,2]{0,1:T(2,128)}, u32[]{:S(2)}) copy-start(s32[189,2]{0,1:T(2,128)} %param.15) | copy-start | bytes 4540
  7.9 0.7 %copy-start.7 = (s32[1,96,4]{1,2,0:T(4,128)S(1)}, s32[1,96,4]{1,2,0:T(4,128)}, u32[]{:S(2)}) copy-start(s32[1,96,4]{1,2,0:T(4,128)} %param.16) | copy-start | bytes 4612
  8.6 0.7 %copy-start.8 = (s32[1,96]{1,0:T(1,128)S(1)}, s32[1,96]{1,0:T(1,128)}, u32[]{:S(2)}) copy-start(s32[1,96]{1,0:T(1,128)} %counts_hbm.1) | copy-start | bytes 1156

commit v4 on v3

--- a/solution.py
+++ b/solution.py
@@ -277,7 +277,7 @@
     )
     return pl.pallas_call(
         kernel,
-        out_shape=jax.ShapeDtypeStruct((1024, K), F32),
+        out_shape=pltpu.VMEM((1024, K), F32),
         in_specs=[pl.BlockSpec(memory_space=pl.ANY)] * 9,
         out_specs=pl.BlockSpec(memory_space=pltpu.VMEM),
         scratch_shapes=[pltpu.VMEM(x.shape, x.dtype) for x in operands]
@@ -305,7 +305,7 @@
         ]
         + [dma] * 6,
         compiler_params=pltpu.CompilerParams(
-            collective_id=0, has_side_effects=True, vmem_limit_bytes=46 * 2**20
+            collective_id=0, has_side_effects=True, vmem_limit_bytes=55 * 2**20
         ),
     )(*operands)
 

time: 58.8 us -> 48.6 us (0.83)
  local copies, waits for them, and re-layouts: 10 us -> 0.8 us
  Pallas kernels: 48.4 us -> 47.7 us
    unnamed x19 -> x1, local copies, waits for them, and re-layouts: 10 us -> 0.8 us
    pallas_call x1, Pallas kernels: 48.4 us -> 47.7 us  [body(): pl.pallas_call(kernel, out_shape=pltpu.VMEM((1024, K), F32), in_specs=[pl...]
where the time goes in v4:
time: 48.6 us; the launch traced here: 48.5 us
  Pallas kernels  47.7 us (98%)
  local copies, waits for them, and re-layouts  0.8 us (2%)
    pallas_call x1, Pallas kernels, body(): pl.pallas_call(kernel, out_shape=pltpu.VMEM((1024, K), F32), in_specs=[pl...  47.7 us

profile of v4, /device:TPU:1, one launch (start us, length us, event | category | flops | bytes accessed | tf_op | source)
XLA Modules:
  0.0 48.5 jit_solution(18163753510733025513)
XLA Ops:
  0.0 47.7 %shard_map.91 = f32[1024,128]{1,0:T(8,128)S(1)} custom-call(bf16[1024,128]{1,0:T(8,128)(2,1)} %mult_hbm.1, bf16[8,128,128]{2,1,0:T(8,128)(2,1)} %up_hbm.1, bf16[8,128,128]{2,1,0:T(8,128)(2,1)} %down_hbm.1, s32[189,128]{1,0:T(8,128)} %src5_hbm.1, s32[16,189]{1,0:T(8,128)} %bitcast.5, s32[2,189]{1,0:T(2,128)} %bitcast.6, s32[4,96]{1,0:T(4,128)} %bitcast.7, ...), custom_call_target="tpu_custom_call" | custom-call | tf_op jit(solution)/shard_map/pallas_call | solution.py:278
  47.7 0.8 %copy.11 = f32[1024,128]{1,0:T(8,128)} copy(f32[1024,128]{1,0:T(8,128)S(1)} %shard_map.91) | data formatting | bytes 1048576

commit v5 on v4

--- a/solution.py
+++ b/solution.py
@@ -19,7 +19,8 @@
 NEAR = 1024
 EMPTY = 1535
 STEP = 63
-BUILD = 63
+SENDS = 5
+BUILD = 10
 STEPS = CLASSES // STEP
 MESH = pl.DeviceIdType.MESH
 F32 = jnp.float32
@@ -127,18 +128,6 @@
     def one_hot(low):
         return jnp.where(lane == jnp.concatenate([low, low], 1), 1.0, 0.0).astype(BF16)
 
-    def build(i, carry):
-        for q in range(BUILD):
-            c = BUILD * i + q
-            hot5[pl.ds(pl.multiple_of(c * 128, 128), 128), :] = one_hot(column(low5[c // 128], c % 128))
-        return carry
-
-    lax.fori_loop(0, CLASSES // BUILD, build, 0)
-    for t in range(2):
-        for h in range(2):
-            hot3[pl.ds((2 * t + h) * 128, 128), :] = one_hot(jnp.bitwise_and(column(idx3[h], t), 255))
-    picks3[...] = jnp.zeros((2048, K), F32)
-
     pl.semaphore_wait(barrier, GROUPS - 1 + SUBS - 1)
 
     def round_group(rows, send, recv):
@@ -161,15 +150,23 @@
 
     slots[g] = pack[g]
 
-    def send_slot(i, carry):
-        j = peer(i)
-        pltpu.make_async_remote_copy(
-            src_ref=pack.at[j], dst_ref=slots.at[g], send_sem=slot_send, recv_sem=slot_recv,
-            device_id=(j, s), device_id_type=MESH,
-        ).start()
+    def send_and_build(i, carry):
+        for q in range(SENDS):
+            j = peer(SENDS * i + q)
+            pltpu.make_async_remote_copy(
+                src_ref=pack.at[j], dst_ref=slots.at[g], send_sem=slot_send, recv_sem=slot_recv,
+                device_id=(j, s), device_id_type=MESH,
+            ).start()
+        for q in range(BUILD):
+            c = BUILD * i + q
+            hot5[pl.ds(pl.multiple_of(c * 128, 128), 128), :] = one_hot(column(low5[c // 128], c % 128))
         return carry
 
-    lax.fori_loop(0, GROUPS - 1, send_slot, 0)
+    lax.fori_loop(0, (GROUPS - 1) // SENDS, send_and_build, 0)
+    for t in range(2):
+        for h in range(2):
+            hot3[pl.ds((2 * t + h) * 128, 128), :] = one_hot(jnp.bitwise_and(column(idx3[h], t), 255))
+    picks3[...] = jnp.zeros((2048, K), F32)
 
     drain(five, 7 * 128, five_send, five_recv).wait_recv()
     four = ascend(five[...], 128, wide, up)
@@ -288,7 +285,7 @@
             pltpu.VMEM((GROUPS, MESSAGE, K), BF16),
             pltpu.VMEM((512, K), BF16),
             pltpu.VMEM((SUBS * SECT, K), BF16),
-            pltpu.VMEM((CLASSES * 128, 256), BF16),
+            pltpu.VMEM(((CLASSES + 1) * 128, 256), BF16),
             pltpu.VMEM((512, 256), BF16),
             pltpu.VMEM((128, CLASSES * K), BF16),
             pltpu.VMEM((128, CLASSES * K), BF16),

time: 48.6 us -> 48.5 us (level)
  no operation moved by 1% of the time
where the time goes in v5:
time: 48.5 us; the launch traced here: 48.4 us
  Pallas kernels  47.6 us (98%)
  local copies, waits for them, and re-layouts  0.8 us (2%)
    pallas_call x1, Pallas kernels, body(): pl.pallas_call(kernel, out_shape=pltpu.VMEM((1024, K), F32), in_specs=[pl...  47.6 us

profile of v5, /device:TPU:1, one launch (start us, length us, event | category | flops | bytes accessed | tf_op | source)
XLA Modules:
  0.0 48.4 jit_solution(4659626346907459716)
XLA Ops:
  0.0 47.6 %shard_map.91 = f32[1024,128]{1,0:T(8,128)S(1)} custom-call(bf16[1024,128]{1,0:T(8,128)(2,1)} %mult_hbm.1, bf16[8,128,128]{2,1,0:T(8,128)(2,1)} %up_hbm.1, bf16[8,128,128]{2,1,0:T(8,128)(2,1)} %down_hbm.1, s32[189,128]{1,0:T(8,128)} %src5_hbm.1, s32[16,189]{1,0:T(8,128)} %bitcast.5, s32[2,189]{1,0:T(2,128)} %bitcast.6, s32[4,96]{1,0:T(4,128)} %bitcast.7, ...), custom_call_target="tpu_custom_call" | custom-call | tf_op jit(solution)/shard_map/pallas_call | solution.py:275
  47.6 0.8 %copy.11 = f32[1024,128]{1,0:T(8,128)} copy(f32[1024,128]{1,0:T(8,128)S(1)} %shard_map.91) | data formatting | bytes 1048576

commit v6 on v5

--- a/solution.py
+++ b/solution.py
@@ -183,14 +183,15 @@
             picked = jnp.where(block == 2 * b, r[:, :K], jnp.where(block == 2 * b + 1, r[:, K:], 0.0))
             picks[:, lanes(c)] = picked.astype(BF16)
 
-    def near(i, carry):
+    def near(i, carry, slots_too=False):
         first = jnp.concatenate([five[0:256, :], five[256:512, :]], 1)
         second = jnp.concatenate([five[512:768, :], five[768:1024, :]], 1)
+        more = [(2, jnp.concatenate([store[0:256, :], store[256:512, :]], 1), picks2)] if slots_too else []
         base = i * STEP
         hot4 = []
         for q in range(STEP):
             c = base + q
-            tiles(c, (0, first, picks0), (1, second, picks1))
+            tiles(c, (0, first, picks0), (1, second, picks1), *more)
             hot4.append(jnp.where(lane4 == column(idx4[c // 128], c % 128), 1.0, 0.0))
         r4 = mm(jnp.concatenate(hot4, 0).astype(BF16), four)
         for q in range(STEP):
@@ -213,7 +214,7 @@
     for copy in round_group(tops.at[pl.ds(section, SECT), :], rest_send, rest_recv):
         copy.start()
 
-    lax.fori_loop(early, CLASSES // STEP, near, 0)
+    lax.fori_loop(early, CLASSES // STEP, functools.partial(near, slots_too=True), 0)
 
     def far(i, carry):
         third = jnp.concatenate([store[0:256, :], store[256:512, :]], 1)
@@ -221,7 +222,7 @@
             tiles(i * STEP + q, (2, third, picks2))
         return carry
 
-    lax.fori_loop(0, CLASSES // STEP, far, 0)
+    lax.fori_loop(0, early, far, 0)
 
     drain(tops, 7 * SECT, rest_send, rest_recv).wait_recv()
     quads = [

time: 48.5 us -> 48.5 us (level)
  no operation moved by 1% of the time
where the time goes in v6:
time: 48.5 us; the launch traced here: 48.4 us
  Pallas kernels  47.6 us (98%)
  local copies, waits for them, and re-layouts  0.8 us (2%)
    pallas_call x1, Pallas kernels, body(): pl.pallas_call(kernel, out_shape=pltpu.VMEM((1024, K), F32), in_specs=[pl...  47.6 us

profile of v6, /device:TPU:1, one launch (start us, length us, event | category | flops | bytes accessed | tf_op | source)
XLA Modules:
  0.0 48.4 jit_solution(17076848864291082477)
XLA Ops:
  0.0 47.6 %shard_map.91 = f32[1024,128]{1,0:T(8,128)S(1)} custom-call(bf16[1024,128]{1,0:T(8,128)(2,1)} %mult_hbm.1, bf16[8,128,128]{2,1,0:T(8,128)(2,1)} %up_hbm.1, bf16[8,128,128]{2,1,0:T(8,128)(2,1)} %down_hbm.1, s32[189,128]{1,0:T(8,128)} %src5_hbm.1, s32[16,189]{1,0:T(8,128)} %bitcast.5, s32[2,189]{1,0:T(2,128)} %bitcast.6, s32[4,96]{1,0:T(4,128)} %bitcast.7, ...), custom_call_target="tpu_custom_call" | custom-call | tf_op jit(solution)/shard_map/pallas_call | solution.py:276
  47.6 0.8 %copy.11 = f32[1024,128]{1,0:T(8,128)} copy(f32[1024,128]{1,0:T(8,128)S(1)} %shard_map.91) | data formatting | bytes 1048576
